TPU v7x, 512 devices: a whole 4x4x16 slice. The times are simulated.
512 devices in a mesh: pop: 8 (over z_hi, x), dp: 4 (over y), tensor: 16 (over z_lo, core).
Axes of the slice: x: 4, y: 4, z: 16 (z_hi: 2, z_lo: 8; z = z_hi * 8 + z_lo), core: 2. Of those that a mesh axis runs over, the one named last changes fastest.
Arguments:
- ranking: int32 [8], replicated, may hold values from 0 to 7, each once
- factor_index: int32 [8, 2, 20], replicated, may hold values from 0 to 2
- weights: bfloat16 [8, 2, 2560, 5120], P('pop', None, 'tensor', 'dp'), may hold values from -0.078125 to 0.078125
- first_moment: float32 [8, 2, 2560, 5120], P('pop', None, 'tensor', 'dp'), may hold values from -12 to 12
- second_moment: float32 [8, 2, 2560, 5120], P('pop', None, 'tensor', 'dp'), may hold values from 1 to 40
- activations: bfloat16 [8, 1024, 5120], P('pop', 'dp', 'tensor')
- cotangent: bfloat16 [8, 1024, 5120], P('pop', 'dp', 'tensor'), may hold values from -6 to 6
Outputs:
- update: bfloat16 [8, 2, 2560, 5120], P('pop', None, 'tensor', 'dp')
Inputs may be any that keep to these rules, and one draw needn't show every extreme that they name: `ranking`: a permutation of the members, best first.
All inputs are finite; a program needn't handle non-finite values.
Results may differ from a plain program's by a relative error of at most 0.012.
Values may be sent and summed in bfloat16 or wider, within the bound.
A program may use at most 128 MiB of HBM per device.

v0:
```python
import jax
import jax.numpy as jnp
from jax import lax
from jax.sharding import PartitionSpec as P

HEAD_SIZE = 128


rate_levels = (0.8, 1.0, 1.25)
beta_one = 0.9
beta_two = 0.95
adam_step = 10
decay = 0.1
epsilon = 1e-08


def pick_rows(pieces, source, members):
    stacked = pieces.reshape(members, -1, pieces.shape[1])
    return jnp.take(stacked, source, axis=0).reshape(pieces.shape)


def copy_joint(weights, first_moment, second_moment, source):
    members = lax.axis_size("pop")
    groups = members * lax.axis_size("tensor")
    arrived = lax.all_to_all(
        pick_rows(
            lax.all_to_all(
                weights.reshape(groups, -1),
                ("pop", "tensor"),
                split_axis=0,
                concat_axis=0,
                tiled=True,
            ),
            source,
            members,
        ),
        ("pop", "tensor"),
        split_axis=0,
        concat_axis=0,
        tiled=True,
    )
    first_new = lax.all_to_all(
        pick_rows(
            lax.all_to_all(
                first_moment.reshape(groups, -1),
                ("pop", "tensor"),
                split_axis=0,
                concat_axis=0,
                tiled=True,
            ),
            source,
            members,
        ),
        ("pop", "tensor"),
        split_axis=0,
        concat_axis=0,
        tiled=True,
    )
    second_new = lax.all_to_all(
        pick_rows(
            lax.all_to_all(
                second_moment.reshape(groups, -1),
                ("pop", "tensor"),
                split_axis=0,
                concat_axis=0,
                tiled=True,
            ),
            source,
            members,
        ),
        ("pop", "tensor"),
        split_axis=0,
        concat_axis=0,
        tiled=True,
    )
    return (
        arrived.reshape(weights.shape),
        first_new.reshape(weights.shape),
        second_new.reshape(weights.shape),
    )


def per_device(ranking, factor_index, weights, first_moment, second_moment, activations, cotangent):
    members = lax.axis_size("pop")
    half_count = members // 2
    member = lax.axis_index("pop")
    source = (
        jnp.zeros((members,), jnp.int32)
        .at[ranking]
        .set(jnp.concatenate([ranking[:half_count], ranking[:half_count]]))
    )
    placed = jnp.zeros((members,), jnp.int32).at[ranking].set(jnp.arange(members, dtype=jnp.int32))
    is_loser = jnp.take(placed, member) >= half_count
    levels = jnp.array(rate_levels, jnp.float32)
    own_index = jnp.take(factor_index, member, axis=0)
    chosen = jnp.sum(
        jnp.where(own_index[..., None] == jnp.arange(3, dtype=jnp.int32), levels, 0.0), axis=-1
    )
    row_count = weights.shape[2]
    head_count = factor_index.shape[2]
    global_rows = lax.axis_index("tensor") * row_count + jnp.arange(row_count, dtype=jnp.int32)
    row_heads = global_rows // HEAD_SIZE
    onehot = (row_heads[:, None] == jnp.arange(head_count, dtype=jnp.int32)[None, :]).astype(
        jnp.float32
    )
    row_factor = jnp.sum(chosen[:, None, :] * onehot[None, :, :], axis=2)
    factor = jnp.where(is_loser, row_factor, 1.0)
    weights, first_moment, second_moment = copy_joint(weights, first_moment, second_moment, source)
    value_weight = weights[0, 0]
    output_weight = weights[0, 1]
    inputs, grads_out = (
        lax.all_gather(activations[0], "tensor", axis=1, tiled=True),
        lax.all_gather(cotangent[0], "tensor", axis=1, tiled=True),
    )
    wide = inputs.astype(jnp.float32)
    normed = (wide * lax.rsqrt(jnp.mean(wide * wide, axis=1, keepdims=True) + 1e-05)).astype(
        jnp.bfloat16
    )
    contract_last = (((1,), (1,)), ((), ()))
    value_part = lax.dot_general(
        normed,
        lax.all_gather(value_weight, "dp", axis=1, tiled=True),
        contract_last,
        preferred_element_type=jnp.float32,
    )
    back_part = lax.dot_general(
        grads_out,
        lax.all_gather(output_weight, "dp", axis=1, tiled=True),
        contract_last,
        preferred_element_type=jnp.float32,
    )
    value_rows = value_part.astype(jnp.bfloat16)
    value_grad = back_part.astype(jnp.bfloat16)
    contract_tokens = (((0,), (0,)), ((), ()))
    first_term = lax.dot_general(
        value_grad, normed, contract_tokens, preferred_element_type=jnp.float32
    )
    second_term = lax.dot_general(
        value_rows, grads_out, contract_tokens, preferred_element_type=jnp.float32
    )
    gradient = lax.psum_scatter(
        jnp.stack([first_term, second_term]).astype(jnp.bfloat16),
        "dp",
        scatter_dimension=2,
        tiled=True,
    ).astype(jnp.float32)
    new_first = beta_one * first_moment[0] + (1.0 - beta_one) * gradient
    new_second = beta_two * second_moment[0] + (1.0 - beta_two) * gradient * gradient
    first_hat = new_first / (1.0 - beta_one**adam_step)
    second_hat = new_second / (1.0 - beta_two**adam_step)
    step_value = -factor[:, :, None] * (
        first_hat / (jnp.sqrt(second_hat) + epsilon) + decay * weights[0].astype(jnp.float32)
    )
    return step_value.astype(jnp.bfloat16)[None]


def solution(mesh):
    in_specs = (
        P(),
        P(),
        P("pop", None, "tensor", "dp"),
        P("pop", None, "tensor", "dp"),
        P("pop", None, "tensor", "dp"),
        P("pop", "dp", "tensor"),
        P("pop", "dp", "tensor"),
    )
    out_specs = P("pop", None, "tensor", "dp")
    return jax.shard_map(
        per_device, mesh=mesh, in_specs=in_specs, out_specs=out_specs, check_vma=False
    )
```

profile of v0, /device:TPU:6, one launch (start us, length us, event | category | flops | bytes accessed | tf_op | source)
XLA Modules:
  0.0 618.5 jit_solution(5673418437638204803)
XLA Ops:
  9.3 5.6 reduce.7
  16.7 19.7 %all-to-all-start.2 = ((bf16[128,2,1600]{2,1,0:T(2,128)(2,1)}), bf16[128,2,1600]{2,1,0:T(2,128)(2,1)S(1)}, u32[]{:S(2)}, u32[]{:S(2)}) async-start(bf16[128,2,1600]{2,1,0:T(2,128)(2,1)} %reshape.275), calls=%async_computation.2 | async-start | bytes 1703936 | tf_op jit(solution)/shard_map/all_to_all | solution.py:27
  39.2 44.4 %all-to-all-done.2 = bf16[128,2,1600]{2,1,0:T(2,128)(2,1)S(1)} async-done(((bf16[128,2,1600]{2,1,0:T(2,128)(2,1)}), bf16[128,2,1600]{2,1,0:T(2,128)(2,1)S(1)}, u32[]{:S(2)}, u32[]{:S(2)}) %all-to-all-start.2) | async-done | bytes 819232 | tf_op jit(solution)/shard_map/all_to_all | solution.py:27
  84.7 7.5 %all-to-all-start = ((f32[128,1,3200]{2,1,0:T(1,128)}), f32[128,1,3200]{2,1,0:T(1,128)S(1)}, u32[]{:S(2)}, u32[]{:S(2)}) async-start(f32[128,1,3200]{2,1,0:T(1,128)} %all_to_all.34), calls=%async_computation | async-start | bytes 3276800 | tf_op jit(solution)/shard_map/all_to_all | solution.py:44
  95.9 88.2 %all-to-all-done = f32[128,1,3200]{2,1,0:T(1,128)S(1)} async-done(((f32[128,1,3200]{2,1,0:T(1,128)}), f32[128,1,3200]{2,1,0:T(1,128)S(1)}, u32[]{:S(2)}, u32[]{:S(2)}) %all-to-all-start) | async-done | bytes 1638432 | tf_op jit(solution)/shard_map/all_to_all | solution.py:44
  184.1 7.0 %all-to-all-start.4 = ((f32[128,1,3200]{2,1,0:T(1,128)}), f32[128,1,3200]{2,1,0:T(1,128)S(1)}, u32[]{:S(2)}, u32[]{:S(2)}) async-start(f32[128,1,3200]{2,1,0:T(1,128)} %all_to_all.41), calls=%async_computation.5 | async-start | bytes 3276800 | tf_op jit(solution)/shard_map/all_to_all | solution.py:61
  192.8 6.4 %reshape.276 = bf16[128,1,3200]{2,1,0:T(2,128)(2,1)} reshape(bf16[128,2,1600]{2,1,0:T(2,128)(2,1)} %copy-done.6) | data formatting | bytes 1638400
  212.8 65.8 %all-to-all-done.4 = f32[128,1,3200]{2,1,0:T(1,128)S(1)} async-done(((f32[128,1,3200]{2,1,0:T(1,128)}), f32[128,1,3200]{2,1,0:T(1,128)S(1)}, u32[]{:S(2)}, u32[]{:S(2)}) %all-to-all-start.4) | async-done | bytes 1638432 | tf_op jit(solution)/shard_map/all_to_all | solution.py:61
  278.6 10.4 %all-to-all-start.3 = ((bf16[128,2,1600]{2,1,0:T(2,128)(2,1)}), bf16[128,2,1600]{2,1,0:T(2,128)(2,1)}, u32[]{:S(2)}, u32[]{:S(2)}) async-start(bf16[128,2,1600]{2,1,0:T(2,128)(2,1)} %reshape.277), calls=%async_computation.3 | async-start | bytes 1703936 | tf_op jit(solution)/shard_map/all_to_all | solution.py:25
  301.2 41.8 %all-to-all-done.3 = bf16[128,2,1600]{2,1,0:T(2,128)(2,1)} async-done(((bf16[128,2,1600]{2,1,0:T(2,128)(2,1)}), bf16[128,2,1600]{2,1,0:T(2,128)(2,1)}, u32[]{:S(2)}, u32[]{:S(2)}) %all-to-all-start.3) | async-done | bytes 819232 | tf_op jit(solution)/shard_map/all_to_all | solution.py:25
  343.0 8.8 %all-to-all-start.1 = ((f32[128,1,3200]{2,1,0:T(1,128)}), f32[128,1,3200]{2,1,0:T(1,128)}, u32[]{:S(2)}, u32[]{:S(2)}) async-start(f32[128,1,3200]{2,1,0:T(1,128)} %all_to_all.36), calls=%async_computation.1 | async-start | bytes 3276800 | tf_op jit(solution)/shard_map/all_to_all | solution.py:42
  351.8 5.5 reshape.278
  357.3 5.0 reduce.1
  367.0 3.9 all_to_all.43
  370.9 55.7 %all-gather.11.cloned.1.call-done = bf16[1,256,5120]{1,2,0:T(8,128)(2,1)} async-done(((bf16[1,256,320]{1,2,0:T(8,128)(2,1)}), bf16[1,256,5120]{1,2,0:T(8,128)(2,1)}) %all-gather.11.cloned.1.call-update) | async-done | bytes 2621456 | tf_op jit(solution)/shard_map/all_gather | solution.py:113
  426.6 32.8 %all-gather.9.cloned.1.call-done = bf16[1,1,160,5120]{3,2,1,0:T(8,128)(2,1)} async-done(((bf16[1,1,160,1280]{3,2,1,0:T(8,128)(2,1)}), bf16[1,1,160,5120]{3,2,1,0:T(8,128)(2,1)}) %all-gather.9.cloned.1.call-update) | async-done | bytes 1638416 | tf_op jit(solution)/shard_map/all_gather | solution.py:128
  459.4 5.6 fusion
  465.1 31.1 %all-gather.15.cloned.1.call-done = bf16[1,1,160,5120]{3,2,1,0:T(8,128)(2,1)} async-done(((bf16[1,1,160,1280]{3,2,1,0:T(8,128)(2,1)}), bf16[1,1,160,5120]{3,2,1,0:T(8,128)(2,1)}) %all-gather.15.cloned.1.call-update) | async-done | bytes 1638416 | tf_op jit(solution)/shard_map/all_gather | solution.py:122
  496.2 5.6 fusion.1
  501.8 16.8 %all-to-all-start.5 = ((f32[128,1,3200]{2,1,0:T(1,128)}), f32[128,1,3200]{2,1,0:T(1,128)S(1)}, u32[]{:S(2)}, u32[]{:S(2)}) async-start(f32[128,1,3200]{2,1,0:T(1,128)} %all_to_all.43), calls=%async_computation.6 | async-start | bytes 3276800 | tf_op jit(solution)/shard_map/all_to_all | solution.py:59
  525.0 6.3 %multiply_reduce_fusion = f32[128,3200]{1,0:T(8,128)} fusion(bf16[128,1,3200]{2,1,0:T(2,128)(2,1)S(1)} %copy-done.2), kind=kLoop, calls=%fused_computation.31 | loop fusion | flops 819200 | bytes 2457600 | tf_op jit(solution)/shard_map/mul | solution.py:152
  533.3 7.5 %multiply_reduce_fusion.2 = f32[128,3200]{1,0:T(8,128)} fusion(f32[128,1,3200]{2,1,0:T(1,128)} %all-to-all-done.1), kind=kLoop, calls=%fused_computation.33 | loop fusion | flops 409600 | bytes 3276800 | tf_op jit(solution)/shard_map/mul | solution.py:147
  543.6 55.3 %all-to-all-done.5 = f32[128,1,3200]{2,1,0:T(1,128)S(1)} async-done(((f32[128,1,3200]{2,1,0:T(1,128)}), f32[128,1,3200]{2,1,0:T(1,128)S(1)}, u32[]{:S(2)}, u32[]{:S(2)}) %all-to-all-start.5) | async-done | bytes 1638432 | tf_op jit(solution)/shard_map/all_to_all | solution.py:59
  598.9 5.9 multiply_reduce_fusion.1
  (77 shorter events, 61.4 us)
Async XLA Ops:
  16.7 19.7 %copy-start.7 = (f32[1,2,160,1280]{3,2,1,0:T(8,128)S(1)}, f32[1,2,160,1280]{3,2,1,0:T(8,128)}, u32[]{:S(2)}) copy-start(f32[1,2,160,1280]{3,2,1,0:T(8,128)} %param.13) | copy-start | bytes 4915204
  16.7 67.0 %all-to-all-start.2 = ((bf16[128,2,1600]{2,1,0:T(2,128)(2,1)}), bf16[128,2,1600]{2,1,0:T(2,128)(2,1)S(1)}, u32[]{:S(2)}, u32[]{:S(2)}) async-start(bf16[128,2,1600]{2,1,0:T(2,128)(2,1)} %reshape.275), calls=%async_computation.2 | async-start | bytes 1703936 | tf_op jit(solution)/shard_map/all_to_all | solution.py:27
  39.2 53.7 %copy-start.8 = (f32[1,2,160,1280]{3,2,1,0:T(8,128)S(1)}, f32[1,2,160,1280]{3,2,1,0:T(8,128)}, u32[]{:S(2)}) copy-start(f32[1,2,160,1280]{3,2,1,0:T(8,128)} %param.14) | copy-start | bytes 4915204
  83.7 1.0 copy-start.6
  84.7 99.4 %all-to-all-start = ((f32[128,1,3200]{2,1,0:T(1,128)}), f32[128,1,3200]{2,1,0:T(1,128)S(1)}, u32[]{:S(2)}, u32[]{:S(2)}) async-start(f32[128,1,3200]{2,1,0:T(1,128)} %all_to_all.34), calls=%async_computation | async-start | bytes 3276800 | tf_op jit(solution)/shard_map/all_to_all | solution.py:44
  92.2 272.4 %all-gather.13.cloned.1.call-start = ((), (), s32[]{:S(2)}) async-start(), calls=%async_computation.10 | async-start | bytes 2785280 | tf_op jit(solution)/shard_map/all_gather | solution.py:112
  95.9 96.0 %copy-start.9 = (s32[8]{0:T(128)S(1)}, s32[8]{0:T(128)}, u32[]{:S(2)}) copy-start(s32[8]{0:T(128)} %param.10) | copy-start | bytes 100
  184.1 94.5 %all-to-all-start.4 = ((f32[128,1,3200]{2,1,0:T(1,128)}), f32[128,1,3200]{2,1,0:T(1,128)S(1)}, u32[]{:S(2)}, u32[]{:S(2)}) async-start(f32[128,1,3200]{2,1,0:T(1,128)} %all_to_all.41), calls=%async_computation.5 | async-start | bytes 3276800 | tf_op jit(solution)/shard_map/all_to_all | solution.py:61
  191.1 235.5 %all-gather.11.cloned.1.call-start = ((), (), s32[]{:S(2)}) async-start(), calls=%async_computation.9 | async-start | bytes 2785280 | tf_op jit(solution)/shard_map/all_gather | solution.py:113
  278.6 64.4 %all-to-all-start.3 = ((bf16[128,2,1600]{2,1,0:T(2,128)(2,1)}), bf16[128,2,1600]{2,1,0:T(2,128)(2,1)}, u32[]{:S(2)}, u32[]{:S(2)}) async-start(bf16[128,2,1600]{2,1,0:T(2,128)(2,1)} %reshape.277), calls=%async_computation.3 | async-start | bytes 1703936 | tf_op jit(solution)/shard_map/all_to_all | solution.py:25
  293.7 1.8 copy-start.5
  343.0 158.8 %all-to-all-start.1 = ((f32[128,1,3200]{2,1,0:T(1,128)}), f32[128,1,3200]{2,1,0:T(1,128)}, u32[]{:S(2)}, u32[]{:S(2)}) async-start(f32[128,1,3200]{2,1,0:T(1,128)} %all_to_all.36), calls=%async_computation.1 | async-start | bytes 3276800 | tf_op jit(solution)/shard_map/all_to_all | solution.py:42
  351.7 107.7 %all-gather.9.cloned.1.call-start = ((), (), s32[]{:S(2)}) async-start(), calls=%async_computation.8 | async-start | bytes 2048000 | tf_op jit(solution)/shard_map/all_gather | solution.py:128
  357.3 5.7 copy-start.1
  364.0 132.2 %all-gather.15.cloned.1.call-start = ((), (), s32[]{:S(2)}) async-start(), calls=%async_computation.11 | async-start | bytes 2048000 | tf_op jit(solution)/shard_map/all_gather | solution.py:122
  367.0 92.4 %copy-start = (bf16[1,256,5120]{1,2,0:T(8,128)(2,1)S(1)}, bf16[1,256,5120]{1,2,0:T(8,128)(2,1)}, u32[]{:S(2)}) copy-start(bf16[1,256,5120]{1,2,0:T(8,128)(2,1)} %all-gather.13.cloned.1.call-done) | copy-start | bytes 7864324
  501.8 16.9 %copy-start.4 = (bf16[1,160,5120]{2,1,0:T(8,128)(2,1)S(1)}, bf16[1,160,5120]{2,1,0:T(8,128)(2,1)}, u32[]{:S(2)}) copy-start(bf16[1,160,5120]{2,1,0:T(8,128)(2,1)} %fusion) | copy-start | bytes 4915204
  501.8 97.1 %all-to-all-start.5 = ((f32[128,1,3200]{2,1,0:T(1,128)}), f32[128,1,3200]{2,1,0:T(1,128)S(1)}, u32[]{:S(2)}, u32[]{:S(2)}) async-start(f32[128,1,3200]{2,1,0:T(1,128)} %all_to_all.43), calls=%async_computation.6 | async-start | bytes 3276800 | tf_op jit(solution)/shard_map/all_to_all | solution.py:59
  518.6 89.2 %reduce-scatter.2.cloned.1.call-start = ((), (), s32[]{:S(2)}) async-start(), calls=%async_computation.7 | async-start | bytes 4096000 | tf_op jit(solution)/shard_map/reduce_scatter | solution.py:141
  522.1 1.9 copy-start.10
  522.1 2.9 copy-start.2
  604.8 3.0 copy-start.3
Sparse Core Ops, SparseCore 0:
  95.1 174.2 all-gather.12
  271.5 155.0 all-gather.10
  428.7 30.6 all-gather.8
  461.4 34.7 all-gather.14
  522.3 46.5 reduce-scatter.1
where the time goes:
time: 628 us; the launch traced here: 618 us
  waiting for transfers between devices  417 us (66%)
  starting transfers between devices  70.6 us (11%)
  local copies, waits for them, and re-layouts  56.3 us (9%)
  other arithmetic  49 us (8%)
  between operations  14.4 us (2%)
  matrix products  11.3 us (2%)
    all_to_all x1, waiting for transfers between devices, copy_joint(): lax.all_to_all(first_moment.reshape(groups, -1), ('pop', 'tensor'), split...  88.2 us
    all_to_all x1, waiting for transfers between devices, copy_joint(): lax.all_to_all(second_moment.reshape(groups, -1), ('pop', 'tensor'), spli...  65.8 us
    all_gather x1, waiting for transfers between devices, per_device(): lax.all_gather(cotangent[0], 'tensor', axis=1, tiled=True)  55.7 us
    all_to_all x1, waiting for transfers between devices, copy_joint(): lax.all_to_all(pick_rows(lax.all_to_all(second_moment.reshape(groups, -1)...  55.3 us
    all_to_all x1, waiting for transfers between devices, copy_joint(): lax.all_to_all(weights.reshape(groups, -1), ('pop', 'tensor'), split_axis...  44.4 us
    all_to_all x1, waiting for transfers between devices, copy_joint(): lax.all_to_all(pick_rows(lax.all_to_all(weights.reshape(groups, -1), ('po...  41.8 us
    all_gather x1, waiting for transfers between devices, per_device(): lax.all_gather(output_weight, 'dp', axis=1, tiled=True)  32.8 us
    all_gather x1, waiting for transfers between devices, per_device(): lax.all_gather(value_weight, 'dp', axis=1, tiled=True)  31.1 us
  transfers between devices with their start and end apart: 11, of which 8 were waited for; matrix products, arithmetic and copies ran while one was open for 14% of the time, Pallas kernels for 0%

commit v1 on v0

v1 whole, which is shorter than its diff:
```python
import functools

import jax
import jax.numpy as jnp
from jax import lax
from jax.experimental import pallas as pl
from jax.experimental.pallas import tpu as pltpu
from jax.sharding import PartitionSpec as P

HEAD_SIZE = 128
HALF = 128
SHIFT = 1.0 / 1024.0

rate_levels = (0.8, 1.0, 1.25)
beta_one = 0.9
beta_two = 0.95
adam_step = 10
decay = 0.1
epsilon = 1e-08
MESH = pl.DeviceIdType.MESH


def kernel(
    n_dp, n_tensor,
    xt_ref, w_ref, m1_ref, m2_ref, fac_ref,
    own_ref, par_ref,
    line, feat, psend, precv, arows, grad,
    xt_sem, left_sem, right_sem, line_sem, loc_sem, y_send, y_recv, sib_send, sib_recv,
    rs_send, rs_recv, ag_send, ag_recv,
):
    j = lax.axis_index("dp")
    i = lax.axis_index("tensor")
    chips = n_tensor // 2
    c = i // 2
    core = i % 2
    sib = c * 2 + 1 - core
    per_row = chips // n_dp
    rounds = xt_ref.shape[0]
    block = xt_ref.shape[2]
    rows = w_ref.shape[1]
    cols = w_ref.shape[2]
    width = n_dp * cols

    def to(dst, src, send, recv, **where):
        return pltpu.make_async_remote_copy(
            src_ref=src, dst_ref=dst, send_sem=send, recv_sem=recv,
            device_id=where, device_id_type=MESH,
        )

    barrier = pltpu.get_barrier_semaphore()
    pl.semaphore_signal(barrier, inc=1, device_id={"tensor": sib}, device_id_type=MESH)
    for k in range(1, n_dp):
        pl.semaphore_signal(
            barrier, inc=1, device_id={"dp": (j + k) % n_dp}, device_id_type=MESH
        )

    @pl.when(c > 0)
    def _():
        pl.semaphore_signal(barrier, inc=1, device_id={"tensor": i - 2}, device_id_type=MESH)

    @pl.when(c < chips - 1)
    def _():
        pl.semaphore_signal(barrier, inc=1, device_id={"tensor": i + 2}, device_id_type=MESH)

    inner = (c > 0) & (c < chips - 1)

    @pl.when(inner)
    def _():
        pl.semaphore_wait(barrier, n_dp + 2)

    @pl.when(jnp.logical_not(inner))
    def _():
        pl.semaphore_wait(barrier, n_dp + 1)

    def place(r, row, q):
        return feat.at[r, row, :, pl.ds(((q % per_row) * 2 + core) * block, block), :]

    def sib_place(r, row, q):
        return feat.at[r, row, :, pl.ds(((q % per_row) * 2 + 1 - core) * block, block), :]

    def go_right(r, q):
        return to(line.at[r, q], line.at[r, q], right_sem.at[r, q], line_sem.at[r, q], tensor=i + 2)

    def go_left(r, q):
        return to(line.at[r, q], line.at[r, q], left_sem.at[r, q], line_sem.at[r, q], tensor=i - 2)

    def keep(r, q):
        return pltpu.make_async_copy(line.at[r, q], place(r, j, q), loc_sem.at[r, q % per_row])

    def keep_sib(r, q):
        return to(
            place(r, j, q), line.at[r, q],
            sib_send.at[r, j, q % per_row], sib_recv.at[r, j, q % per_row], tensor=sib,
        )

    def across(r, q):
        return to(
            place(r, j, q), line.at[r, q],
            y_send.at[r, q], y_recv.at[r, j, q % per_row], dp=q // per_row,
        )

    def arrive(r, row, q):
        return to(
            place(r, row, q), place(r, row, q),
            y_send.at[r, q], y_recv.at[r, row, q % per_row], dp=row,
        )

    def pass_sib(r, row, q):
        return to(
            place(r, row, q), place(r, row, q),
            sib_send.at[r, row, q % per_row], sib_recv.at[r, row, q % per_row], tensor=sib,
        )

    def from_sib(r, row, q):
        return to(
            sib_place(r, row, q), sib_place(r, row, q),
            sib_send.at[r, row, q % per_row], sib_recv.at[r, row, q % per_row], tensor=sib,
        )

    def deliver(r, q):
        @pl.when(q // per_row == j)
        def _():
            keep_sib(r, q).start()
            keep(r, q).start()

        @pl.when(q // per_row != j)
        def _():
            across(r, q).start()

    def own_sends(r):
        @pl.when(c < chips - 1)
        def _():
            go_right(r, c).start()

        @pl.when(c > 0)
        def _():
            go_left(r, c).start()

        deliver(r, c)

    def collect(r, q):
        @pl.when(q // per_row == j)
        def _():
            for k in range(1, n_dp):
                row = (j + k) % n_dp
                arrive(r, row, q).wait_recv()
                pass_sib(r, row, q).start()

    def line_step(r, s):
        @pl.when((s >= 1) & (c - s >= 0))
        def _():
            q = c - s
            go_right(r, q).wait_recv()

            @pl.when(c < chips - 1)
            def _():
                go_right(r, q).start()

            deliver(r, q)

        @pl.when((s >= 1) & (c + s < chips))
        def _():
            q = c + s
            go_left(r, q).wait_recv()

            @pl.when(c > 0)
            def _():
                go_left(r, q).start()

            deliver(r, q)

        @pl.when(s == 1)
        def _():
            collect(r, c)

        @pl.when((s >= 2) & (c - s + 1 >= 0))
        def _():
            collect(r, c - s + 1)

        @pl.when((s >= 2) & (c + s - 1 < chips))
        def _():
            collect(r, c + s - 1)

    def rs_copy(r, peer):
        return to(
            precv.at[r, j], psend.at[r, peer], rs_send.at[r, peer], rs_recv.at[r, j], dp=peer
        )

    def rs_arrive(r, peer):
        return to(
            precv.at[r, peer], psend.at[r, peer], rs_send.at[r, peer], rs_recv.at[r, peer], dp=peer
        )

    def ag_copy(r, peer):
        return to(
            arows.at[r, j], arows.at[r, j], ag_send.at[r, peer], ag_recv.at[r, j], dp=peer
        )

    def ag_arrive(r, peer):
        return to(
            arows.at[r, peer], arows.at[r, peer], ag_send.at[r, peer], ag_recv.at[r, peer], dp=peer
        )

    def joined(r, a):
        return jnp.concatenate([feat[r, row, a] for row in range(n_dp)], axis=1)

    def products(r):
        for row in range(n_dp):
            for k in range(per_row):
                from_sib(r, row, k).wait_recv()
        for k in range(per_row):
            keep(r, j * per_row + k).wait()
        for a in range(2):
            part = jnp.dot(w_ref[a], joined(r, a), preferred_element_type=jnp.float32)
            for row in range(n_dp):
                psend[r, row, a * rows:(a + 1) * rows, :] = part[
                    :, row * HALF:(row + 1) * HALF
                ].astype(jnp.bfloat16)
        for row in range(n_dp):
            wide = feat[r, row, 0].astype(jnp.float32)
            total = jnp.sum(wide * wide, axis=0, keepdims=True) * SHIFT
            high = total.astype(jnp.bfloat16)
            low = jnp.where(total < 1e37, total - high.astype(jnp.float32), 0.0)
            psend[r, row, 2 * rows:2 * rows + 16, :] = jnp.concatenate(
                [high.astype(jnp.float32), low, jnp.zeros((14, HALF), jnp.float32)], axis=0
            ).astype(jnp.bfloat16)
        for k in range(1, n_dp):
            rs_copy(r, (j + k) % n_dp).start()

    def reduce(r):
        acc = psend[r, j].astype(jnp.float32)
        for k in range(1, n_dp):
            row = (j + k) % n_dp
            rs_arrive(r, row).wait_recv()
            acc = acc + precv[r, row].astype(jnp.float32)
        total = acc[2 * rows:2 * rows + 1] + acc[2 * rows + 1:2 * rows + 2]
        scale = lax.rsqrt(total * (1.0 / (SHIFT * width)) + 1e-05)
        live = scale > 0.0
        arows[r, j, 0] = jnp.where(live, acc[rows:2 * rows] * scale, 0.0).astype(jnp.bfloat16)
        arows[r, j, 1] = jnp.where(live, acc[:rows] * scale, 0.0).astype(jnp.bfloat16)
        for k in range(1, n_dp):
            ag_copy(r, (j + k) % n_dp).start()

    def gradients(r):
        for k in range(1, n_dp):
            ag_arrive(r, (j + k) % n_dp).wait_recv()
        for a in range(2):
            mine = jnp.concatenate([arows[r, row, a] for row in range(n_dp)], axis=1)
            part = lax.dot_general(
                mine, joined(r, a), (((1,), (1,)), ((), ())), preferred_element_type=jnp.float32
            )
            grad[a] = jnp.where(r % 2 == 0, part, grad[a] + part)

    def adam(a, tile):
        here = pl.ds(pl.multiple_of(tile * 128, 128), 128)
        gradient = grad[a, :, here]
        new_first = beta_one * m1_ref[a, :, here] + (1.0 - beta_one) * gradient
        new_second = beta_two * m2_ref[a, :, here] + (1.0 - beta_two) * gradient * gradient
        first_hat = new_first / (1.0 - beta_one**adam_step)
        second_hat = new_second / (1.0 - beta_two**adam_step)
        return here, (
            first_hat / (jnp.sqrt(second_hat) + epsilon)
            + decay * w_ref[a, :, here].astype(jnp.float32)
        )

    tiles = cols // 128

    def update_own():
        for a in range(2):
            def one(tile, carry):
                here, step = adam(a, tile)
                own_ref[a, :, here] = (-step).astype(jnp.bfloat16)
                return carry

            lax.fori_loop(0, tiles, one, 0)

    def update_partner():
        half = rows // 2
        for a in range(2):
            factor = -fac_ref[a]

            def one(tile, carry):
                _, step = adam(a, tile)
                step = (factor * step).astype(jnp.bfloat16)
                par_ref[a * 2 * tiles + tile] = step[:half]
                par_ref[(a * 2 + 1) * tiles + tile] = step[half:]
                return carry

            lax.fori_loop(0, tiles, one, 0)

    for r in range(rounds):
        pltpu.make_async_copy(xt_ref.at[r], line.at[r, c], xt_sem.at[r]).start()
    for r in range(rounds):
        pltpu.make_async_copy(xt_ref.at[r], line.at[r, c], xt_sem.at[r]).wait()
    own_sends(0)

    def turn(r, carry):
        def one(s, carry):
            @pl.when(r < rounds)
            def _():
                line_step(r, s)

            @pl.when((r + 1 < rounds) & (s == chips // 2))
            def _():
                own_sends(r + 1)

            @pl.when((r > 0) & (s == 2))
            def _():
                products(r - 1)

            @pl.when((r > 0) & (s == chips // 2))
            def _():
                reduce(r - 1)

            @pl.when((r > 0) & (s == chips - 2))
            def _():
                gradients(r - 1)

            return carry

        lax.fori_loop(1, chips + 1, one, 0)

        @pl.when(r == 2)
        def _():
            update_own()

        return carry

    lax.fori_loop(0, rounds + 1, turn, 0)
    update_partner()

    def drain(r, carry):
        def one(q, carry):
            @pl.when((q <= c) & (c < chips - 1))
            def _():
                go_right(r, q).wait_send()

            @pl.when((q >= c) & (c > 0))
            def _():
                go_left(r, q).wait_send()

            @pl.when(q // per_row != j)
            def _():
                across(r, q).wait_send()

            return carry

        lax.fori_loop(0, chips, one, 0)
        for row in range(n_dp):
            for k in range(per_row):
                pass_sib(r, row, k).wait_send()
        for k in range(1, n_dp):
            peer = (j + k) % n_dp
            rs_copy(r, peer).wait_send()
            ag_copy(r, peer).wait_send()
        return carry

    lax.fori_loop(0, rounds, drain, 0)


def exploit_step(xt, weights, first_moment, second_moment, factor):
    n_dp, n_tensor = lax.axis_size("dp"), lax.axis_size("tensor")
    rounds, _, block, _ = xt.shape
    _, rows, cols = weights.shape
    chips = n_tensor // 2
    per_row = chips // n_dp
    dma = pltpu.SemaphoreType.DMA
    vmem = pl.BlockSpec(memory_space=pltpu.VMEM)
    half_tiles = 2 * 2 * (cols // 128)
    flops = rounds * 2 * 2 * 2 * rows * cols * n_dp * HALF
    return pl.pallas_call(
        functools.partial(kernel, n_dp, n_tensor),
        out_shape=(
            jax.ShapeDtypeStruct((2, rows, cols), jnp.bfloat16),
            jax.ShapeDtypeStruct((half_tiles, rows // 2, 128), jnp.bfloat16),
        ),
        in_specs=[vmem] * 5,
        out_specs=(vmem, vmem),
        scratch_shapes=[
            pltpu.VMEM((rounds, chips, 2, block, HALF), jnp.bfloat16),
            pltpu.VMEM((rounds, n_dp, 2, cols, HALF), jnp.bfloat16),
            pltpu.VMEM((rounds, n_dp, 2 * rows + 16, HALF), jnp.bfloat16),
            pltpu.VMEM((rounds, n_dp, 2 * rows + 16, HALF), jnp.bfloat16),
            pltpu.VMEM((rounds, n_dp, 2, rows, HALF), jnp.bfloat16),
            pltpu.VMEM((2, rows, cols), jnp.float32),
            dma((rounds,)),
            dma((rounds, chips)),
            dma((rounds, chips)),
            dma((rounds, chips)),
            dma((rounds, per_row)),
            dma((rounds, chips)),
            dma((rounds, n_dp, per_row)),
            dma((rounds, n_dp, per_row)),
            dma((rounds, n_dp, per_row)),
            dma((rounds, n_dp)),
            dma((rounds, n_dp)),
            dma((rounds, n_dp)),
            dma((rounds, n_dp)),
        ],
        compiler_params=pltpu.CompilerParams(
            collective_id=0, has_side_effects=True, vmem_limit_bytes=56 * 1024 * 1024
        ),
        cost_estimate=pl.CostEstimate(
            flops=flops, bytes_accessed=8 * rows * cols * 4, transcendentals=0
        ),
        name="gather_and_step",
    )(xt, weights, first_moment, second_moment, factor)


def swap(pieces, chosen):
    arrived = lax.all_to_all(pieces, "pop", split_axis=0, concat_axis=0, tiled=True)
    picked = jnp.take(arrived, chosen, axis=0)
    return lax.all_to_all(picked, "pop", split_axis=0, concat_axis=0, tiled=True)


def per_device(ranking, factor_index, weights, first_moment, second_moment, activations, cotangent):
    members = lax.axis_size("pop")
    half_count = members // 2
    member = lax.axis_index("pop")
    winners, losers = ranking[:half_count], ranking[half_count:]
    partner = (
        jnp.zeros((members,), jnp.int32).at[winners].set(losers).at[losers].set(winners)
    )
    placed = jnp.zeros((members,), jnp.int32).at[ranking].set(jnp.arange(members, dtype=jnp.int32))
    is_loser = jnp.take(placed, member) >= half_count
    levels = jnp.array(rate_levels, jnp.float32)
    partner_index = jnp.take(factor_index, jnp.take(partner, member), axis=0)
    chosen = jnp.sum(
        jnp.where(partner_index[..., None] == jnp.arange(3, dtype=jnp.int32), levels, 0.0), axis=-1
    )
    row_count = weights.shape[2]
    head_count = factor_index.shape[2]
    global_rows = lax.axis_index("tensor") * row_count + jnp.arange(row_count, dtype=jnp.int32)
    row_heads = global_rows // HEAD_SIZE
    onehot = (row_heads[:, None] == jnp.arange(head_count, dtype=jnp.int32)[None, :]).astype(
        jnp.float32
    )
    row_factor = jnp.sum(chosen[:, None, :] * onehot[None, :, :], axis=2)

    tokens, block = activations.shape[1:]
    both = jnp.stack([activations[0], cotangent[0]])
    own = both.reshape(2, 2, HALF, block).transpose(1, 0, 3, 2)
    other = swap(own.reshape(members, -1, HALF), partner).reshape(own.shape)
    own_step, partner_step = exploit_step(
        jnp.concatenate([own, other]),
        weights[0], first_moment[0], second_moment[0], row_factor[:, :, None],
    )
    rows, cols = weights.shape[2:]
    tiles = partner_step.shape[0]
    returned = swap(partner_step.reshape(members, tiles // members, rows // 2, 128), partner)
    returned = (
        returned.reshape(2, 2, cols // 128, rows // 2, 128)
        .transpose(0, 1, 3, 2, 4)
        .reshape(2, rows, cols)
    )
    return jnp.where(is_loser, returned, own_step)[None]


def solution(mesh):
    in_specs = (
        P(),
        P(),
        P("pop", None, "tensor", "dp"),
        P("pop", None, "tensor", "dp"),
        P("pop", None, "tensor", "dp"),
        P("pop", "dp", "tensor"),
        P("pop", "dp", "tensor"),
    )
    out_specs = P("pop", None, "tensor", "dp")
    return jax.shard_map(
        per_device, mesh=mesh, in_specs=in_specs, out_specs=out_specs, check_vma=False
    )
```

time: 628 us -> 332 us (0.53); the launches traced: 618 us -> 331 us
  waiting for transfers between devices: 417 us -> 41.4 us
  Pallas kernels: 0 us -> 195 us
  local copies, waits for them, and re-layouts: 56.3 us -> 6.37 us
  blocking collectives: 0 us -> 47.6 us
  other arithmetic: 49 us -> 6.52 us
  starting transfers between devices: 70.6 us -> 33.1 us
  between operations: 14.4 us -> 1.31 us
  matrix products: 11.3 us -> 0 us
    all_to_all x6 -> x3, waiting for transfers between devices: 296 us -> 41.4 us  [the longest x2 28.2 us: swap(): lax.all_to_all(picked, 'pop', split_axis=0, concat_axis=0, tiled=True)]
    pallas_call x0 -> x1, Pallas kernels: none -> 195 us  [exploit_step(): pl.pallas_call(functools.partial(kernel, n_dp, n_tensor), out_shape=(jax....]
    all_gather x4 -> x0, waiting for transfers between devices: 120 us -> none  [the longest x1 55.7 us: per_device(): lax.all_gather(cotangent[0], 'tensor', axis=1, tiled=True)]
    all_to_all x0 -> x1, blocking collectives: none -> 47.6 us  [swap(): lax.all_to_all(pieces, 'pop', split_axis=0, concat_axis=0, tiled=True)]
    all_to_all x6 -> x3, starting transfers between devices: 70.2 us -> 33.1 us  [the longest x1 18 us: swap(): lax.all_to_all(pieces, 'pop', split_axis=0, concat_axis=0, tiled=True)]
    unnamed x29 -> x6, local copies, waits for them, and re-layouts: 21.9 us -> 0.31 us
    mul x3 -> x0, other arithmetic: 19.7 us -> none  [the longest x1 7.48 us: per_device(): new_first = beta_one * first_moment[0] + (1.0 - beta_one) * gradient]
    all_to_all x6 -> x0, local copies, waits for them, and re-layouts: 15.1 us -> none  [the longest x1 3.88 us: copy_joint(): lax.all_to_all(pick_rows(lax.all_to_all(second_moment.reshape(groups, -1)...]
  transfers between devices with their start and end apart: 11 -> 3, of which waited for: 8 -> 3; matrix products, arithmetic and copies ran while one was open for 14% -> 1% of each run, Pallas kernels for 0% -> 0%
where the time goes in v1:
time: 332 us; the launch traced here: 331 us
  Pallas kernels  195 us (59%)
  blocking collectives  47.6 us (14%)
  waiting for transfers between devices  41.4 us (12%)
  starting transfers between devices  33.1 us (10%)
  other arithmetic  6.52 us (2%)
  local copies, waits for them, and re-layouts  6.37 us (2%)
    pallas_call x1, Pallas kernels, exploit_step(): pl.pallas_call(functools.partial(kernel, n_dp, n_tensor), out_shape=(jax....  195 us
    all_to_all x1, blocking collectives, swap(): lax.all_to_all(pieces, 'pop', split_axis=0, concat_axis=0, tiled=True)  47.6 us
    all_to_all x2, waiting for transfers between devices, swap(): lax.all_to_all(picked, 'pop', split_axis=0, concat_axis=0, tiled=True)  28.2 us
    all_to_all x1, starting transfers between devices, swap(): lax.all_to_all(pieces, 'pop', split_axis=0, concat_axis=0, tiled=True)  18 us
    all_to_all x2, starting transfers between devices, swap(): lax.all_to_all(picked, 'pop', split_axis=0, concat_axis=0, tiled=True)  15 us
    all_to_all x1, waiting for transfers between devices, swap(): lax.all_to_all(pieces, 'pop', split_axis=0, concat_axis=0, tiled=True)  13.3 us
  transfers between devices with their start and end apart: 3, of which 3 were waited for; matrix products, arithmetic and copies ran while one was open for 1% of the time, Pallas kernels for 0%

profile of v1, /device:TPU:6, one launch (start us, length us, event | category | flops | bytes accessed | tf_op | source)
XLA Modules:
  0.0 331.1 jit_solution(8208958250778866280)
XLA Ops:
  0.0 1.8 fusion.6
  1.8 18.0 %all-to-all-start = ((bf16[8,160,128]{2,1,0:T(8,128)(2,1)}), bf16[8,160,128]{2,1,0:T(8,128)(2,1)S(1)}, u32[]{:S(2)}, u32[]{:S(2)}) async-start(bf16[8,160,128]{2,1,0:T(8,128)(2,1)} %bitcast.3), calls=%async_computation | async-start | bytes 655360 | tf_op jit(solution)/shard_map/all_to_all | solution.py:411
  19.9 0.6 scatter_custom_fusion.1
  20.5 0.6 scatter_fusion
  21.1 13.3 %all-to-all-done = bf16[8,160,128]{2,1,0:T(8,128)(2,1)S(1)} async-done(((bf16[8,160,128]{2,1,0:T(8,128)(2,1)}), bf16[8,160,128]{2,1,0:T(8,128)(2,1)S(1)}, u32[]{:S(2)}, u32[]{:S(2)}) %all-to-all-start) | async-done | bytes 327712 | tf_op jit(solution)/shard_map/all_to_all | solution.py:411
  34.4 0.6 gather_fusion
  35.0 0.8 broadcast_select_fusion.1
  35.8 5.8 %all-to-all-start.1 = ((bf16[8,160,128]{2,1,0:T(8,128)(2,1)}), bf16[8,160,128]{2,1,0:T(8,128)(2,1)S(1)}, u32[]{:S(2)}, u32[]{:S(2)}) async-start(bf16[8,160,128]{2,1,0:T(8,128)(2,1)} %broadcast_select_fusion.1), calls=%async_computation.1 | async-start | bytes 655360 | tf_op jit(solution)/shard_map/all_to_all | solution.py:413
  41.7 0.6 dynamic-slice.8
  42.8 0.7 select_bitcast_fusion.1
  43.8 0.8 copy.17.fac_ref
  44.6 11.0 %all-to-all-done.1 = bf16[8,160,128]{2,1,0:T(8,128)(2,1)S(1)} async-done(((bf16[8,160,128]{2,1,0:T(8,128)(2,1)}), bf16[8,160,128]{2,1,0:T(8,128)(2,1)S(1)}, u32[]{:S(2)}, u32[]{:S(2)}) %all-to-all-start.1) | async-done | bytes 327712 | tf_op jit(solution)/shard_map/all_to_all | solution.py:413
  55.6 0.9 pad_maximum_fusion.xt_ref
  56.5 194.8 %gather_and_step.1 = (bf16[2,160,1280]{2,1,0:T(8,128)(2,1)}, bf16[40,80,128]{2,1,0:T(8,128)(2,1)}) custom-call(bf16[4,2,320,128]{3,2,1,0:T(8,128)(2,1)} %pad_maximum_fusion.xt_ref, bf16[2,160,1280]{2,1,0:T(8,128)(2,1)} %bitcast.36, f32[2,160,1280]{2,1,0:T(8,128)} %bitcast.34, f32[2,160,1280]{2,1,0:T(8,128)} %bitcast.35, f32[2,160,1]{2,1,0:T(8,128)} %copy.17.fac_ref), custom_call_target="tpu_custom_call" | custom-call | flops 3355443200 | bytes 6553600 | tf_op jit(solution)/shard_map/gather_and_step/pallas_call | solution.py:371
  251.3 47.6 %all_to_all.20 = bf16[8,5,80,128]{3,2,1,0:T(8,128)(2,1)S(1)} all-to-all(bf16[8,5,80,128]{3,2,1,0:T(8,128)(2,1)} %bitcast.32), channel_id=1, replica_groups=mesh['pop'=8,'dp'=4,'tensor'=16] {'pop'}, dimensions={0} | all-to-all | bytes 1638400 | tf_op jit(solution)/shard_map/all_to_all | solution.py:411
  298.9 0.7 gather_fusion.1
  299.6 1.0 broadcast_select_fusion
  300.6 9.2 %all-to-all-start.3 = ((bf16[8,5,80,128]{3,2,1,0:T(8,128)(2,1)}), bf16[8,5,80,128]{3,2,1,0:T(8,128)(2,1)S(1)}, u32[]{:S(2)}, u32[]{:S(2)}) async-start(bf16[8,5,80,128]{3,2,1,0:T(8,128)(2,1)} %broadcast_select_fusion), calls=%async_computation.3 | async-start | bytes 1638400 | tf_op jit(solution)/shard_map/all_to_all | solution.py:413
  309.8 0.6 scatter_custom_fusion
  310.4 0.7 dynamic-slice.7
  311.7 17.2 %all-to-all-done.3 = bf16[8,5,80,128]{3,2,1,0:T(8,128)(2,1)S(1)} async-done(((bf16[8,5,80,128]{3,2,1,0:T(8,128)(2,1)}), bf16[8,5,80,128]{3,2,1,0:T(8,128)(2,1)S(1)}, u32[]{:S(2)}, u32[]{:S(2)}) %all-to-all-start.3) | async-done | bytes 819232 | tf_op jit(solution)/shard_map/all_to_all | solution.py:413
  329.3 0.5 reshape.73
  329.8 0.3 copy-done
  330.1 1.0 select_bitcast_fusion
  (17 shorter events, 0.7 us)
Async XLA Ops:
  0.0 19.8 %copy-start.1 = (s32[8]{0:T(128)S(1)}, s32[8]{0:T(128)}, u32[]{:S(2)}) copy-start(s32[8]{0:T(128)} %param.8) | copy-start | bytes 100
  1.8 32.6 %all-to-all-start = ((bf16[8,160,128]{2,1,0:T(8,128)(2,1)}), bf16[8,160,128]{2,1,0:T(8,128)(2,1)S(1)}, u32[]{:S(2)}, u32[]{:S(2)}) async-start(bf16[8,160,128]{2,1,0:T(8,128)(2,1)} %bitcast.3), calls=%async_computation | async-start | bytes 655360 | tf_op jit(solution)/shard_map/all_to_all | solution.py:411
  19.8 23.7 %copy-start.2 = (f32[3]{0:T(128)S(1)}, f32[3]{0:T(128)}, u32[]{:S(2)}) copy-start(f32[3]{0:T(128)} %constant.97.clone) | copy-start | bytes 40
  35.8 19.7 %all-to-all-start.1 = ((bf16[8,160,128]{2,1,0:T(8,128)(2,1)}), bf16[8,160,128]{2,1,0:T(8,128)(2,1)S(1)}, u32[]{:S(2)}, u32[]{:S(2)}) async-start(bf16[8,160,128]{2,1,0:T(8,128)(2,1)} %broadcast_select_fusion.1), calls=%async_computation.1 | async-start | bytes 655360 | tf_op jit(solution)/shard_map/all_to_all | solution.py:413
  300.6 28.3 %all-to-all-start.3 = ((bf16[8,5,80,128]{3,2,1,0:T(8,128)(2,1)}), bf16[8,5,80,128]{3,2,1,0:T(8,128)(2,1)S(1)}, u32[]{:S(2)}, u32[]{:S(2)}) async-start(bf16[8,5,80,128]{3,2,1,0:T(8,128)(2,1)} %broadcast_select_fusion), calls=%async_computation.3 | async-start | bytes 1638400 | tf_op jit(solution)/shard_map/all_to_all | solution.py:413
  329.0 1.1 copy-start

commit v2 on v1

v2 whole, which is shorter than its diff:
```python
import functools

import jax
import jax.numpy as jnp
from jax import lax
from jax.experimental import pallas as pl
from jax.experimental.pallas import tpu as pltpu
from jax.sharding import PartitionSpec as P

HEAD_SIZE = 128
HALF = 128
SHIFT = 1.0 / 1024.0

rate_levels = (0.8, 1.0, 1.25)
beta_one = 0.9
beta_two = 0.95
adam_step = 10
decay = 0.1
epsilon = 1e-08
MESH = pl.DeviceIdType.MESH


def kernel(
    n_cross, n_pop, n_dp, n_tensor,
    table, xt_ref, w_ref, m1_ref, m2_ref, fac_ref,
    out_ref,
    near0, near1, near2, far0, far1, far2, sent, back, short, w_new, m_new,
    feat, psend, precv, arows, grad,
    loc_sem, y_send, y_recv, left_sem, right_sem, line_sem, sib_send, sib_recv,
    rs_send, rs_recv, ag_send, ag_recv,
    near_send, near_recv, far_send, far_recv, back_send, back_recv,
):
    p = lax.axis_index("pop")
    n_x = n_pop // 2
    side = p // n_x
    x = p % n_x
    opposite = (p + n_x) % n_pop
    j = lax.axis_index("dp")
    i = lax.axis_index("tensor")
    chips = n_tensor // 2
    c = i // 2
    core = i % 2
    sib = c * 2 + 1 - core
    per_row = chips // n_dp
    rounds = feat.shape[0]
    block = xt_ref.shape[2]
    rows = w_ref.shape[1]
    cols = w_ref.shape[2]
    width = n_dp * cols
    steps = per_row * n_dp
    home = c // per_row
    mine = c % per_row

    def to(dst, src, send, recv, **where):
        return pltpu.make_async_remote_copy(
            src_ref=src, dst_ref=dst, send_sem=send, recv_sem=recv,
            device_id=where, device_id_type=MESH,
        )

    barrier = pltpu.get_barrier_semaphore()
    pl.semaphore_signal(barrier, inc=1, device_id={"tensor": sib}, device_id_type=MESH)
    for k in range(1, n_dp):
        pl.semaphore_signal(
            barrier, inc=1, device_id={"dp": (j + k) % n_dp}, device_id_type=MESH
        )
    for k in range(1, n_x):
        pl.semaphore_signal(
            barrier, inc=1, device_id={"pop": side * n_x + (x + k) % n_x}, device_id_type=MESH
        )
    pl.semaphore_signal(barrier, inc=1, device_id={"pop": opposite}, device_id_type=MESH)

    @pl.when(c > 0)
    def _():
        pl.semaphore_signal(barrier, inc=1, device_id={"tensor": i - 2}, device_id_type=MESH)

    @pl.when(c < chips - 1)
    def _():
        pl.semaphore_signal(barrier, inc=1, device_id={"tensor": i + 2}, device_id_type=MESH)

    inner = (c > 0) & (c < chips - 1)

    @pl.when(inner)
    def _():
        pl.semaphore_wait(barrier, n_dp + n_x + 2)

    @pl.when(jnp.logical_not(inner))
    def _():
        pl.semaphore_wait(barrier, n_dp + n_x + 1)

    def place(r, row, k, half):
        return feat.at[r, row, :, pl.ds((k * 2 + half) * block, block), :]

    def keep(r, src):
        return pltpu.make_async_copy(src, place(r, j, mine, core), loc_sem.at[r])

    def across(r, src):
        return to(place(r, j, mine, core), src, y_send.at[r], y_recv.at[r, j], dp=home)

    def arrive(r, row):
        here = place(r, row, mine, core)
        return to(here, here, y_send.at[r], y_recv.at[r, row], dp=row)

    def go_right(r, k, row):
        here = place(r, row, k, core)
        return to(here, here, right_sem.at[r, k, row], line_sem.at[r, k, row], tensor=i + 2)

    def go_left(r, k, row):
        here = place(r, row, k, core)
        return to(here, here, left_sem.at[r, k, row], line_sem.at[r, k, row], tensor=i - 2)

    def pass_sib(r, k, row):
        here = place(r, row, k, core)
        return to(here, here, sib_send.at[r, k, row], sib_recv.at[r, k, row], tensor=sib)

    def from_sib(r, k, row):
        here = place(r, row, k, 1 - core)
        return to(here, here, sib_send.at[r, k, row], sib_recv.at[r, k, row], tensor=sib)

    def spread(r):
        @pl.when(home == j)
        def _():
            keep(r, xt_ref.at[r]).start()

        @pl.when(home != j)
        def _():
            across(r, xt_ref.at[r]).start()

    def line_step(r, n):
        first = jnp.where(c <= j * per_row, 0, 1)
        k = jnp.where(n < n_dp, first, 1 - first)
        row = (j + n) % n_dp
        start = j * per_row + k

        @pl.when((start == c) & (row == j))
        def _():
            keep(r, place(r, j, mine, core)).wait()

        @pl.when((start == c) & (row != j))
        def _():
            arrive(r, row).wait_recv()

        @pl.when(start < c)
        def _():
            go_right(r, k, row).wait_recv()

        @pl.when(start > c)
        def _():
            go_left(r, k, row).wait_recv()

        @pl.when((start <= c) & (c < chips - 1))
        def _():
            go_right(r, k, row).start()

        @pl.when((start >= c) & (c > 0))
        def _():
            go_left(r, k, row).start()

        pass_sib(r, k, row).start()

    def rs_copy(r, peer):
        return to(
            precv.at[r, j], psend.at[r, peer], rs_send.at[r, peer], rs_recv.at[r, j], dp=peer
        )

    def rs_arrive(r, peer):
        return to(
            precv.at[r, peer], psend.at[r, peer], rs_send.at[r, peer], rs_recv.at[r, peer], dp=peer
        )

    def ag_copy(r, peer):
        return to(
            arows.at[r, j], arows.at[r, j], ag_send.at[r, peer], ag_recv.at[r, j], dp=peer
        )

    def ag_arrive(r, peer):
        return to(
            arows.at[r, peer], arows.at[r, peer], ag_send.at[r, peer], ag_recv.at[r, peer], dp=peer
        )

    def joined(r, a):
        return jnp.concatenate([feat[r, row, a] for row in range(n_dp)], axis=1)

    def products(r, a):
        part = jnp.dot(w_new[a], joined(r, a), preferred_element_type=jnp.float32)
        for row in range(n_dp):
            psend[r, row, a * rows:(a + 1) * rows, :] = part[
                :, row * HALF:(row + 1) * HALF
            ].astype(jnp.bfloat16)

    def first_products(r):
        for k in range(per_row):
            for row in range(n_dp):
                from_sib(r, k, row).wait_recv()
        products(r, 0)

    def second_products(r):
        products(r, 1)
        for row in range(n_dp):
            wide = feat[r, row, 0].astype(jnp.float32)
            total = jnp.sum(wide * wide, axis=0, keepdims=True) * SHIFT
            high = total.astype(jnp.bfloat16)
            low = jnp.where(total < 1e37, total - high.astype(jnp.float32), 0.0)
            psend[r, row, 2 * rows:2 * rows + 16, :] = jnp.concatenate(
                [high.astype(jnp.float32), low, jnp.zeros((14, HALF), jnp.float32)], axis=0
            ).astype(jnp.bfloat16)
        for k in range(1, n_dp):
            rs_copy(r, (j + k) % n_dp).start()

    def reduce(r):
        acc = psend[r, j].astype(jnp.float32)
        for k in range(1, n_dp):
            row = (j + k) % n_dp
            rs_arrive(r, row).wait_recv()
            acc = acc + precv[r, row].astype(jnp.float32)
        total = acc[2 * rows:2 * rows + 1] + acc[2 * rows + 1:2 * rows + 2]
        scale = lax.rsqrt(total * (1.0 / (SHIFT * width)) + 1e-05)
        live = scale > 0.0
        arows[r, j, 0] = jnp.where(live, acc[rows:2 * rows] * scale, 0.0).astype(jnp.bfloat16)
        arows[r, j, 1] = jnp.where(live, acc[:rows] * scale, 0.0).astype(jnp.bfloat16)
        for k in range(1, n_dp):
            ag_copy(r, (j + k) % n_dp).start()

    def gradients(r, a):
        mixed = jnp.concatenate([arows[r, row, a] for row in range(n_dp)], axis=1)
        part = lax.dot_general(
            mixed, joined(r, a), (((1,), (1,)), ((), ())), preferred_element_type=jnp.float32
        )
        if r == 0:
            grad[a] = part
        else:
            grad[a] = grad[a] + part

    def first_gradients(r):
        for k in range(1, n_dp):
            ag_arrive(r, (j + k) % n_dp).wait_recv()
        gradients(r, 0)

    def second_gradients(r):
        gradients(r, 1)

    def update():
        for a in range(2):
            factor = -fac_ref[a]

            def one(tile, carry):
                here = pl.ds(pl.multiple_of(tile * 128, 128), 128)
                gradient = grad[a, :, here]
                first = m_new[0, a, :, here].astype(jnp.float32)
                second = m_new[1, a, :, here].astype(jnp.float32)
                new_first = beta_one * first + (1.0 - beta_one) * gradient
                new_second = beta_two * second + (1.0 - beta_two) * gradient * gradient
                first_hat = new_first / (1.0 - beta_one**adam_step)
                second_hat = new_second / (1.0 - beta_two**adam_step)
                step = first_hat / (jnp.sqrt(second_hat) + epsilon) + decay * w_new[
                    a, :, here
                ].astype(jnp.float32)
                out_ref[a, :, here] = (factor * step).astype(jnp.bfloat16)
                return carry

            lax.fori_loop(0, cols // 128, one, 0)

    near = (near0, near1, near2)
    far = (far0, far1, far2)
    parts = n_x // 2
    size = rows // parts

    def piece(ref, q):
        return ref.at[q // parts, pl.ds(q % parts * size, size), :]

    def held(ch):
        return w_ref if ch == 0 else short.at[ch - 1]

    def new(ch):
        return w_new if ch == 0 else m_new.at[ch - 1]

    def others(f):
        for k in range(1, n_x):
            f((x + k) % n_x)

    def near_copy(ch, q):
        return to(
            near[ch].at[x], piece(held(ch), q), near_send.at[ch, q], near_recv.at[ch, x],
            pop=side * n_x + q,
        )

    def near_arrive(ch, q):
        here = near[ch].at[q]
        return to(here, here, near_send.at[ch, q], near_recv.at[ch, q], pop=side * n_x + q)

    def far_copy(ch, s):
        return to(
            far[ch].at[s], sent.at[ch, s], far_send.at[ch, s], far_recv.at[ch, s], pop=opposite
        )

    def back_copy(ch, q):
        return to(
            piece(new(ch), x), back.at[ch, q], back_send.at[ch, q], back_recv.at[ch, x],
            pop=side * n_x + q,
        )

    def back_arrive(ch, q):
        here = piece(new(ch), q)
        return to(here, here, back_send.at[ch, q], back_recv.at[ch, q], pop=side * n_x + q)

    def near_out(ch):
        others(lambda q: near_copy(ch, q).start())
        near[ch][x] = piece(held(ch), x)[...]

    def far_out(ch):
        others(lambda q: near_arrive(ch, q).wait_recv())
        for s in range(n_cross):
            sent[ch, s] = near[ch][table[s]]
            far_copy(ch, s).start()

    def back_out(ch):
        for s in range(n_cross):
            far_copy(ch, s).wait_recv()
        for q in range(n_x):
            pick = table[n_x + q]
            got = near[ch][jnp.minimum(pick, n_x - 1)]
            if n_cross:
                got = jnp.where(pick < n_x, got, far[ch][jnp.maximum(pick - n_x, 0)])
            back[ch, q] = got
        others(lambda q: back_copy(ch, q).start())
        piece(new(ch), x)[...] = back[ch, x]

    def back_in(ch):
        others(lambda q: back_arrive(ch, q).wait_recv())

    def moments(f):
        def go():
            f(1)
            f(2)

        return go

    near_out(0)
    spread(0)
    spread(1)
    for a in range(2):
        short[0, a] = m1_ref[a].astype(jnp.bfloat16)
        short[1, a] = m2_ref[a].astype(jnp.bfloat16)
    moments(near_out)()

    whole = rounds * steps
    eighth = whole // 8
    work = [(eighth, lambda: far_out(0))]
    if n_cross == 0:
        work += [
            (eighth, lambda: back_out(0)),
            (3 * eighth, moments(far_out)),
            (3 * eighth, moments(back_out)),
        ]
    elif n_cross == 1:
        work += [(5 * eighth, lambda: back_out(0)), (6 * eighth - 1, moments(far_out))]
    elif n_cross == 2:
        work += [(3 * eighth, moments(far_out)), (whole - 1, lambda: back_out(0))]
    else:
        work += [(3 * eighth, moments(far_out))]

    def turn(f, carry):
        line_step(f // steps, f % steps)
        for at, part in work:
            @pl.when(f == at)
            def _():
                part()

        return carry

    lax.fori_loop(0, whole, turn, 0)
    if n_cross > 2:
        back_out(0)
    back_in(0)
    for r in range(rounds):
        first_products(r)
        second_products(r)
    for r in range(rounds):
        reduce(r)
    first_gradients(0)
    second_gradients(0)
    if n_cross:
        moments(back_out)()
    first_gradients(1)
    second_gradients(1)
    moments(back_in)()
    update()

    def drain(r, carry):
        for k in range(per_row):
            start = j * per_row + k

            @pl.when((start <= c) & (c < chips - 1))
            def _():
                for row in range(n_dp):
                    go_right(r, k, row).wait_send()

            @pl.when((start >= c) & (c > 0))
            def _():
                for row in range(n_dp):
                    go_left(r, k, row).wait_send()

            for row in range(n_dp):
                pass_sib(r, k, row).wait_send()
        for k in range(1, n_dp):
            peer = (j + k) % n_dp
            rs_copy(r, peer).wait_send()
            ag_copy(r, peer).wait_send()

        @pl.when(home != j)
        def _():
            across(r, xt_ref.at[r]).wait_send()

        return carry

    lax.fori_loop(0, rounds, drain, 0)
    for ch in range(3):
        others(lambda q: near_copy(ch, q).wait_send())
        others(lambda q: back_copy(ch, q).wait_send())
        for s in range(n_cross):
            far_copy(ch, s).wait_send()


def exploit_step(n_cross, table, xt, weights, first_moment, second_moment, factor):
    n_pop, n_dp, n_tensor = (lax.axis_size(name) for name in ("pop", "dp", "tensor"))
    rounds = xt.shape[0]
    block = xt.shape[2]
    _, rows, cols = weights.shape
    chips = n_tensor // 2
    per_row = chips // n_dp
    n_x = n_pop // 2
    slots = max(n_cross, 1)
    dma = pltpu.SemaphoreType.DMA
    vmem = pl.BlockSpec(memory_space=pltpu.VMEM)
    bf16 = functools.partial(pltpu.VMEM, dtype=jnp.bfloat16)
    part = (4 * rows // n_pop, cols)
    flops = rounds * 2 * 2 * 2 * rows * cols * n_dp * HALF
    return pl.pallas_call(
        functools.partial(kernel, n_cross, n_pop, n_dp, n_tensor),
        out_shape=jax.ShapeDtypeStruct((2, rows, cols), jnp.bfloat16),
        in_specs=[pl.BlockSpec(memory_space=pltpu.SMEM)] + [vmem] * 5,
        out_specs=vmem,
        scratch_shapes=[bf16((n_x,) + part)] * 3
        + [bf16((slots,) + part)] * 3
        + [
            bf16((3, slots) + part),
            bf16((3, n_x) + part),
            bf16((2, 2, rows, cols)),
            bf16((2, rows, cols)),
            bf16((2, 2, rows, cols)),
            bf16((rounds, n_dp, 2, cols, HALF)),
            bf16((rounds, n_dp, 2 * rows + 16, HALF)),
            bf16((rounds, n_dp, 2 * rows + 16, HALF)),
            bf16((rounds, n_dp, 2, rows, HALF)),
            pltpu.VMEM((2, rows, cols), jnp.float32),
            dma((rounds,)),
            dma((rounds,)),
            dma((rounds, n_dp)),
            dma((rounds, per_row, n_dp)),
            dma((rounds, per_row, n_dp)),
            dma((rounds, per_row, n_dp)),
            dma((rounds, per_row, n_dp)),
            dma((rounds, per_row, n_dp)),
            dma((rounds, n_dp)),
            dma((rounds, n_dp)),
            dma((rounds, n_dp)),
            dma((rounds, n_dp)),
            dma((3, n_x)),
            dma((3, n_x)),
            dma((3, slots)),
            dma((3, slots)),
            dma((3, n_x)),
            dma((3, n_x)),
        ],
        compiler_params=pltpu.CompilerParams(
            collective_id=n_cross, has_side_effects=True, vmem_limit_bytes=56 * 1024 * 1024
        ),
        cost_estimate=pl.CostEstimate(
            flops=flops, bytes_accessed=8 * rows * cols * 4, transcendentals=0
        ),
        name=f"exploit_{n_cross}",
    )(table, xt, weights, first_moment, second_moment, factor)


def plan(ranking, side):
    members = ranking.shape[0]
    n_x = members // 2
    ids = jnp.arange(members, dtype=jnp.int32)
    placed = (ranking[:, None] == ids[None, :]).astype(jnp.int32)
    from_rank = jnp.concatenate([ranking[:n_x], ranking[:n_x]])
    source = jnp.sum(placed * from_rank[:, None], axis=0)
    loser = jnp.sum(placed[n_x:], axis=0)
    crosses = (source // n_x != ids // n_x).astype(jnp.int32)
    before = (ids[:, None] < ids[None, :]) & (ids[:, None] // n_x == ids[None, :] // n_x)
    slot = jnp.sum(crosses[:, None] * before, axis=0)
    n_cross = jnp.maximum(jnp.sum(crosses[:n_x]), jnp.sum(crosses[n_x:]))
    picks = jnp.where(crosses > 0, n_x + slot, source % n_x)
    use = (crosses > 0) & (ids // n_x != side)
    sends = jnp.sum(
        jnp.where(use[None, :] & (slot[None, :] == ids[:n_x, None]), source % n_x, 0), axis=1
    )
    mine = jnp.where(side > 0, picks[n_x:], picks[:n_x])
    return loser, n_cross, jnp.concatenate([sends, mine])


def per_device(ranking, factor_index, weights, first_moment, second_moment, activations, cotangent):
    members = lax.axis_size("pop")
    member = lax.axis_index("pop")
    loser, n_cross, table = plan(ranking, member // (members // 2))
    is_loser = jnp.sum(jnp.where(jnp.arange(members) == member, loser, 0)) > 0
    levels = jnp.array(rate_levels, jnp.float32)
    own_index = jnp.take(factor_index, member, axis=0)
    chosen = jnp.sum(
        jnp.where(own_index[..., None] == jnp.arange(3, dtype=jnp.int32), levels, 0.0), axis=-1
    )
    row_count = weights.shape[2]
    head_count = factor_index.shape[2]
    global_rows = lax.axis_index("tensor") * row_count + jnp.arange(row_count, dtype=jnp.int32)
    row_heads = global_rows // HEAD_SIZE
    onehot = (row_heads[:, None] == jnp.arange(head_count, dtype=jnp.int32)[None, :]).astype(
        jnp.float32
    )
    row_factor = jnp.sum(chosen[:, None, :] * onehot[None, :, :], axis=2)
    factor = jnp.where(is_loser, row_factor, 1.0)[:, :, None]

    block = activations.shape[2]
    both = jnp.stack([activations[0], cotangent[0]])
    own = both.reshape(2, 2, HALF, block).transpose(1, 0, 3, 2)
    step = lax.switch(
        n_cross,
        [functools.partial(exploit_step, k) for k in range(members // 2 + 1)],
        table, own, weights[0], first_moment[0], second_moment[0], factor,
    )
    return step[None]


def solution(mesh):
    in_specs = (
        P(),
        P(),
        P("pop", None, "tensor", "dp"),
        P("pop", None, "tensor", "dp"),
        P("pop", None, "tensor", "dp"),
        P("pop", "dp", "tensor"),
        P("pop", "dp", "tensor"),
    )
    out_specs = P("pop", None, "tensor", "dp")
    return jax.shard_map(
        per_device, mesh=mesh, in_specs=in_specs, out_specs=out_specs, check_vma=False
    )
```

time: 332 us -> 266 us (0.80)
  Pallas kernels: 195 us -> 254 us
  blocking collectives: 47.6 us -> 0 us
  waiting for transfers between devices: 41.4 us -> 0 us
  starting transfers between devices: 33.1 us -> 0 us
  local copies, waits for them, and re-layouts: 6.37 us -> 2.65 us
    pallas_call x1, Pallas kernels: 195 us -> 254 us  [exploit_step(): pl.pallas_call(functools.partial(kernel, n_cross, n_pop, n_dp, n_tensor),...]
    all_to_all x1 -> x0, blocking collectives: 47.6 us -> none  [swap(): lax.all_to_all(pieces, 'pop', split_axis=0, concat_axis=0, tiled=True)]
    all_to_all x3 -> x0, waiting for transfers between devices: 41.4 us -> none  [the longest x2 28.2 us: swap(): lax.all_to_all(picked, 'pop', split_axis=0, concat_axis=0, tiled=True)]
    all_to_all x3 -> x0, starting transfers between devices: 33.1 us -> none  [the longest x1 18 us: swap(): lax.all_to_all(pieces, 'pop', split_axis=0, concat_axis=0, tiled=True)]
  transfers between devices with their start and end apart: 3 -> 0, of which waited for: 3 -> 0; matrix products, arithmetic and copies ran while one was open for 1% -> 0% of each run, Pallas kernels for 0% -> 0%
where the time goes in v2:
time: 266 us
  Pallas kernels  254 us (95%)
  other arithmetic  6.8 us (3%)
    pallas_call x1, Pallas kernels, exploit_step(): pl.pallas_call(functools.partial(kernel, n_cross, n_pop, n_dp, n_tensor),...  254 us

profile of v2, /device:TPU:6, one launch (start us, length us, event | category | flops | bytes accessed | tf_op | source)
XLA Modules:
  0.0 266.0 jit_solution(8080380846493123402)
XLA Ops:
  0.0 0.8 pad_add_fusion
  0.8 0.7 select_reduce_fusion.1
  1.6 0.1 select_reduce_fusion
  1.7 0.2 select_reduce_fusion.2
  1.9 0.1 broadcast_select_fusion
  2.0 0.1 pad_add_fusion.1
  2.0 0.8 slice_reduce_fusion.5
  4.2 0.7 fusion.11
  4.9 1.0 pad_maximum_fusion
  5.9 0.1 reshape.266
  6.0 259.0 %conditional.1 = (bf16[1,2,160,1280]{3,2,1,0:T(8,128)(2,1)S(1)}) conditional(s32[]{:T(128)} %clamp.3, (bf16[1,2,160,1280]{3,2,1,0:T(8,128)(2,1)}, f32[1,2,160,1280]{3,2,1,0:T(8,128)}, f32[1,2,160,1280]{3,2,1,0:T(8,128)}, s32[]{:T(128)}, s32[8]{0:T(128)S(1)}, /*index=5*/s32[8,8]{1,0:T(8,128)S(1)}, s32[8]{0:T(128)S(1)}, ...), branch_computations={%region_5.10_spmd.clone, %region_10.15_spmd.clone, %region_15.20_s... | conditional | flops 1677734784 | bytes 7230105 | solution.py:528
  6.1 0.7 select_bitcast_fusion.5
  6.8 0.8 copy.111.xt_ref
  7.5 0.7 fusion.4
  8.3 0.7 fusion.5
  9.7 0.1 copy.103
  9.8 0.1 multiply_reduce_fusion.2
  9.9 0.8 copy.104.fac_ref
  10.7 253.9 %exploit_2.2 = bf16[2,160,1280]{2,1,0:T(8,128)(2,1)S(1)} custom-call(s32[8]{0:T(128)S(1)} %get-tuple-element.791.table, bf16[2,2,320,128]{3,2,1,0:T(8,128)(2,1)} %copy.111.xt_ref, bf16[2,160,1280]{2,1,0:T(8,128)(2,1)} %bitcast.79, f32[2,160,1280]{2,1,0:T(8,128)} %bitcast.69, f32[2,160,1280]{2,1,0:T(8,128)} %bitcast.74, f32[2,160,1]{2,1,0:T(8,128)} %copy.104.fac_ref), custom_call_target="tpu_custom_call" | custom-call | flops 1677721600 | bytes 6553600 | tf_op jit(solution)/shard_map/cond/branch_2_fun/exploit_2/pallas_call | solution.py:437
  265.1 0.9 copy.120
  (11 shorter events, 0.1 us)

commit v3 on v2

--- a/solution.py
+++ b/solution.py
@@ -21,20 +21,23 @@
 
 
 def kernel(
-    n_cross, n_pop, n_dp, n_tensor,
-    table, xt_ref, w_ref, m1_ref, m2_ref, fac_ref,
+    counts, n_pop, n_dp, n_tensor, n_heads,
+    rank_ref, choice_ref, act_ref, cot_ref, w_ref, m1_ref, m2_ref,
     out_ref,
-    near0, near1, near2, far0, far1, far2, sent, back, short, w_new, m_new,
+    xt_ref, wide1, wide2, near0, near1, near2, far0, far1, far2, sent, back, short, w_new, m_new,
     feat, psend, precv, arows, grad,
     loc_sem, y_send, y_recv, left_sem, right_sem, line_sem, sib_send, sib_recv,
     rs_send, rs_recv, ag_send, ag_recv,
-    near_send, near_recv, far_send, far_recv, back_send, back_recv,
+    near_send, near_recv, far_send, far_recv, back_send, back_recv, own_sem,
 ):
     p = lax.axis_index("pop")
     n_x = n_pop // 2
     side = p // n_x
     x = p % n_x
     opposite = (p + n_x) % n_pop
+    n_cross = max(counts)
+    n_sent = jnp.where(side == 0, counts[0], counts[1])
+    n_got = jnp.where(side == 0, counts[1], counts[0])
     j = lax.axis_index("dp")
     i = lax.axis_index("tensor")
     chips = n_tensor // 2
@@ -51,6 +54,9 @@
     home = c // per_row
     mine = c % per_row
 
+    for m, (ref, wide) in enumerate(((m1_ref, wide1), (m2_ref, wide2))):
+        pltpu.make_async_copy(ref, wide, own_sem.at[m]).start()
+
     def to(dst, src, send, recv, **where):
         return pltpu.make_async_remote_copy(
             src_ref=src, dst_ref=dst, send_sem=send, recv_sem=recv,
@@ -77,6 +83,47 @@
     def _():
         pl.semaphore_signal(barrier, inc=1, device_id={"tensor": i + 2}, device_id_type=MESH)
 
+    sends = [jnp.int32(0)] * max(n_cross, 1)
+    picks = [jnp.int32(q) for q in range(n_x)]
+    losing = jnp.int32(0)
+    arrived = [jnp.int32(0), jnp.int32(0)]
+    for pair in range(n_x):
+        winner, loser = rank_ref[pair], rank_ref[n_x + pair]
+        w_side, l_side = lax.div(winner, n_x), lax.div(loser, n_x)
+        w_x = winner - w_side * n_x
+        cross = w_side != l_side
+        slot = jnp.where(l_side > 0, arrived[1], arrived[0])
+        arrived = [
+            arrived[0] + jnp.where(cross & (l_side == 0), 1, 0),
+            arrived[1] + jnp.where(cross & (l_side > 0), 1, 0),
+        ]
+        sends = [
+            jnp.where(cross & (w_side == side) & (slot == n), w_x, old)
+            for n, old in enumerate(sends)
+        ]
+        picks = [
+            jnp.where(loser == side * n_x + q, jnp.where(cross, n_x + slot, w_x), old)
+            for q, old in enumerate(picks)
+        ]
+        losing = jnp.where(loser == p, 1, losing)
+
+    def levels(a, head):
+        choice = choice_ref[(p * 2 + a) * n_heads + jnp.minimum(head, n_heads - 1)]
+        level = jnp.where(
+            choice == 0, rate_levels[0], jnp.where(choice == 1, rate_levels[1], rate_levels[2])
+        )
+        return jnp.where(losing > 0, level, 1.0)
+
+    def row_factor(a):
+        first_row = i * rows
+        head = first_row // HEAD_SIZE
+        at = lax.broadcasted_iota(jnp.int32, (rows, 128), 0) + (first_row - head * HEAD_SIZE)
+        return jnp.where(
+            at < HEAD_SIZE,
+            levels(a, head),
+            jnp.where(at < 2 * HEAD_SIZE, levels(a, head + 1), levels(a, head + 2)),
+        )
+
     inner = (c > 0) & (c < chips - 1)
 
     @pl.when(inner)
@@ -100,21 +147,28 @@
         here = place(r, row, mine, core)
         return to(here, here, y_send.at[r], y_recv.at[r, row], dp=row)
 
-    def go_right(r, k, row):
-        here = place(r, row, k, core)
-        return to(here, here, right_sem.at[r, k, row], line_sem.at[r, k, row], tensor=i + 2)
-
-    def go_left(r, k, row):
-        here = place(r, row, k, core)
-        return to(here, here, left_sem.at[r, k, row], line_sem.at[r, k, row], tensor=i - 2)
-
-    def pass_sib(r, k, row):
-        here = place(r, row, k, core)
-        return to(here, here, sib_send.at[r, k, row], sib_recv.at[r, k, row], tensor=sib)
-
-    def from_sib(r, k, row):
-        here = place(r, row, k, 1 - core)
-        return to(here, here, sib_send.at[r, k, row], sib_recv.at[r, k, row], tensor=sib)
+    def place_of(r, row, k, half, a):
+        return feat.at[r, row, a, pl.ds((k * 2 + half) * block, block), :]
+
+    def go_right(r, k, row, a):
+        here = place_of(r, row, k, core, a)
+        at = (r, k, row, a)
+        return to(here, here, right_sem.at[at], line_sem.at[at], tensor=i + 2)
+
+    def go_left(r, k, row, a):
+        here = place_of(r, row, k, core, a)
+        at = (r, k, row, a)
+        return to(here, here, left_sem.at[at], line_sem.at[at], tensor=i - 2)
+
+    def pass_sib(r, k, row, a):
+        here = place_of(r, row, k, core, a)
+        at = (r, k, row, a)
+        return to(here, here, sib_send.at[at], sib_recv.at[at], tensor=sib)
+
+    def from_sib(r, k, row, a):
+        here = place_of(r, row, k, 1 - core, a)
+        at = (r, k, row, a)
+        return to(here, here, sib_send.at[at], sib_recv.at[at], tensor=sib)
 
     def spread(r):
         @pl.when(home == j)
@@ -125,37 +179,37 @@
         def _():
             across(r, xt_ref.at[r]).start()
 
-    def line_step(r, n):
+    def line_step(r, n, a):
         first = jnp.where(c <= j * per_row, 0, 1)
         k = jnp.where(n < n_dp, first, 1 - first)
         row = (j + n) % n_dp
         start = j * per_row + k
 
-        @pl.when((start == c) & (row == j))
+        @pl.when((start == c) & (row == j) & (a == 0))
         def _():
             keep(r, place(r, j, mine, core)).wait()
 
-        @pl.when((start == c) & (row != j))
+        @pl.when((start == c) & (row != j) & (a == 0))
         def _():
             arrive(r, row).wait_recv()
 
         @pl.when(start < c)
         def _():
-            go_right(r, k, row).wait_recv()
+            go_right(r, k, row, a).wait_recv()
 
         @pl.when(start > c)
         def _():
-            go_left(r, k, row).wait_recv()
+            go_left(r, k, row, a).wait_recv()
 
         @pl.when((start <= c) & (c < chips - 1))
         def _():
-            go_right(r, k, row).start()
+            go_right(r, k, row, a).start()
 
         @pl.when((start >= c) & (c > 0))
         def _():
-            go_left(r, k, row).start()
-
-        pass_sib(r, k, row).start()
+            go_left(r, k, row, a).start()
+
+        pass_sib(r, k, row, a).start()
 
     def rs_copy(r, peer):
         return to(
@@ -190,7 +244,8 @@
     def first_products(r):
         for k in range(per_row):
             for row in range(n_dp):
-                from_sib(r, k, row).wait_recv()
+                for a in range(2):
+                    from_sib(r, k, row, a).wait_recv()
         products(r, 0)
 
     def second_products(r):
@@ -240,7 +295,7 @@
 
     def update():
         for a in range(2):
-            factor = -fac_ref[a]
+            factor = -row_factor(a)
 
             def one(tile, carry):
                 here = pl.ds(pl.multiple_of(tile * 128, 128), 128)
@@ -304,85 +359,83 @@
 
     def near_out(ch):
         others(lambda q: near_copy(ch, q).start())
-        near[ch][x] = piece(held(ch), x)[...]
+        if ch == 0:
+            own_weights().start()
+        else:
+            near[ch][x] = piece(held(ch), x)[...]
+
+    def own_weights():
+        return pltpu.make_async_copy(piece(w_ref, x), near[0].at[x], own_sem.at[2])
 
     def far_out(ch):
+        if ch == 0:
+            own_weights().wait()
         others(lambda q: near_arrive(ch, q).wait_recv())
         for s in range(n_cross):
-            sent[ch, s] = near[ch][table[s]]
-            far_copy(ch, s).start()
+            @pl.when(s < n_sent)
+            def _():
+                sent[ch, s] = near[ch][sends[s]]
+                far_copy(ch, s).start()
 
     def back_out(ch):
         for s in range(n_cross):
-            far_copy(ch, s).wait_recv()
+            @pl.when(s < n_got)
+            def _():
+                far_copy(ch, s).wait_recv()
+
         for q in range(n_x):
-            pick = table[n_x + q]
-            got = near[ch][jnp.minimum(pick, n_x - 1)]
-            if n_cross:
-                got = jnp.where(pick < n_x, got, far[ch][jnp.maximum(pick - n_x, 0)])
-            back[ch, q] = got
+            back[ch, q] = near[ch][jnp.minimum(picks[q], n_x - 1)]
+
+        if n_cross:
+            @pl.when(n_got > 0)
+            def _():
+                for q in range(n_x):
+                    got = far[ch][jnp.maximum(picks[q] - n_x, 0)]
+                    back[ch, q] = jnp.where(picks[q] < n_x, back[ch, q], got)
+
         others(lambda q: back_copy(ch, q).start())
         piece(new(ch), x)[...] = back[ch, x]
 
     def back_in(ch):
         others(lambda q: back_arrive(ch, q).wait_recv())
 
-    def moments(f):
-        def go():
-            f(1)
-            f(2)
-
-        return go
-
     near_out(0)
-    spread(0)
-    spread(1)
-    for a in range(2):
-        short[0, a] = m1_ref[a].astype(jnp.bfloat16)
-        short[1, a] = m2_ref[a].astype(jnp.bfloat16)
-    moments(near_out)()
-
-    whole = rounds * steps
-    eighth = whole // 8
-    work = [(eighth, lambda: far_out(0))]
-    if n_cross == 0:
-        work += [
-            (eighth, lambda: back_out(0)),
-            (3 * eighth, moments(far_out)),
-            (3 * eighth, moments(back_out)),
-        ]
-    elif n_cross == 1:
-        work += [(5 * eighth, lambda: back_out(0)), (6 * eighth - 1, moments(far_out))]
-    elif n_cross == 2:
-        work += [(3 * eighth, moments(far_out)), (whole - 1, lambda: back_out(0))]
-    else:
-        work += [(3 * eighth, moments(far_out))]
+    for u in range(2):
+        for a, ref in enumerate((act_ref, cot_ref)):
+            xt_ref[u, a] = ref[u * HALF:(u + 1) * HALF, :].T
+        spread(u)
+    for m, wide in enumerate((wide1, wide2)):
+        pltpu.make_async_copy(wide, wide, own_sem.at[m]).wait()
+        for a in range(2):
+            short[m, a] = wide[a].astype(jnp.bfloat16)
+        near_out(m + 1)
+
+    whole = rounds * steps * 2
+    parts_of = {
+        "far": far_out, "back": back_out, "in": back_in,
+        "prod": lambda r: (first_products(r), second_products(r)),
+        "sum": reduce,
+        "grad": lambda r: (first_gradients(r), second_gradients(r)),
+    }
+
+    def run(name):
+        parts_of[name[:-1]](int(name[-1]))
+
+    during, after = schedule(*counts)
 
     def turn(f, carry):
-        line_step(f // steps, f % steps)
-        for at, part in work:
-            @pl.when(f == at)
+        line_step(f // (2 * steps), f // 2 % steps, f % 2)
+        for at, names in during:
+            @pl.when(f == at * whole // 16)
             def _():
-                part()
+                for name in names:
+                    run(name)
 
         return carry
 
     lax.fori_loop(0, whole, turn, 0)
-    if n_cross > 2:
-        back_out(0)
-    back_in(0)
-    for r in range(rounds):
-        first_products(r)
-        second_products(r)
-    for r in range(rounds):
-        reduce(r)
-    first_gradients(0)
-    second_gradients(0)
-    if n_cross:
-        moments(back_out)()
-    first_gradients(1)
-    second_gradients(1)
-    moments(back_in)()
+    for name in after:
+        run(name)
     update()
 
     def drain(r, carry):
@@ -392,15 +445,18 @@
             @pl.when((start <= c) & (c < chips - 1))
             def _():
                 for row in range(n_dp):
-                    go_right(r, k, row).wait_send()
+                    for a in range(2):
+                        go_right(r, k, row, a).wait_send()
 
             @pl.when((start >= c) & (c > 0))
             def _():
                 for row in range(n_dp):
-                    go_left(r, k, row).wait_send()
+                    for a in range(2):
+                        go_left(r, k, row, a).wait_send()
 
             for row in range(n_dp):
-                pass_sib(r, k, row).wait_send()
+                for a in range(2):
+                    pass_sib(r, k, row, a).wait_send()
         for k in range(1, n_dp):
             peer = (j + k) % n_dp
             rs_copy(r, peer).wait_send()
@@ -417,29 +473,65 @@
         others(lambda q: near_copy(ch, q).wait_send())
         others(lambda q: back_copy(ch, q).wait_send())
         for s in range(n_cross):
-            far_copy(ch, s).wait_send()
-
-
-def exploit_step(n_cross, table, xt, weights, first_moment, second_moment, factor):
+            @pl.when(s < n_sent)
+            def _():
+                far_copy(ch, s).wait_send()
+
+
+def schedule(there, back):
+    if there + back == 0:
+        return (
+            (
+                (2, ("far0", "back0")),
+                (6, ("far1", "far2", "back1", "back2")),
+                (12, ("in0",)),
+                (14, ("prod0",)),
+            ),
+            ("prod1", "sum0", "sum1", "grad0", "grad1", "in1", "in2"),
+        )
+    compute = ("prod0", "prod1", "sum0", "sum1")
+    if there == back == 1:
+        return (
+            ((2, ("far0",)), (10, ("back0",))),
+            ("far1", "far2", "in0") + compute
+            + ("back1", "grad0", "grad1", "back2", "in1", "in2"),
+        )
+    return (
+        ((2, ("far0",)),),
+        ("far1", "far2", "back0", "in0") + compute
+        + ("grad0", "grad1", "back1", "back2", "in1", "in2"),
+    )
+
+
+def exploit_step(counts, ranking, choice, activations, cotangent, weights, first, second):
     n_pop, n_dp, n_tensor = (lax.axis_size(name) for name in ("pop", "dp", "tensor"))
-    rounds = xt.shape[0]
-    block = xt.shape[2]
+    rounds = 2
+    block = activations.shape[1]
     _, rows, cols = weights.shape
     chips = n_tensor // 2
     per_row = chips // n_dp
     n_x = n_pop // 2
-    slots = max(n_cross, 1)
+    slots = max(counts + (1,))
     dma = pltpu.SemaphoreType.DMA
+    smem = pl.BlockSpec(memory_space=pltpu.SMEM)
     vmem = pl.BlockSpec(memory_space=pltpu.VMEM)
+    hbm = pl.BlockSpec(memory_space=pl.ANY)
     bf16 = functools.partial(pltpu.VMEM, dtype=jnp.bfloat16)
     part = (4 * rows // n_pop, cols)
     flops = rounds * 2 * 2 * 2 * rows * cols * n_dp * HALF
     return pl.pallas_call(
-        functools.partial(kernel, n_cross, n_pop, n_dp, n_tensor),
+        functools.partial(
+            kernel, counts, n_pop, n_dp, n_tensor, choice.shape[0] // (2 * n_pop)
+        ),
         out_shape=jax.ShapeDtypeStruct((2, rows, cols), jnp.bfloat16),
-        in_specs=[pl.BlockSpec(memory_space=pltpu.SMEM)] + [vmem] * 5,
+        in_specs=[smem, smem, vmem, vmem, hbm, hbm, hbm],
         out_specs=vmem,
-        scratch_shapes=[bf16((n_x,) + part)] * 3
+        scratch_shapes=[
+            bf16((rounds, 2, block, HALF)),
+            pltpu.VMEM((2, rows, cols), jnp.float32),
+            pltpu.VMEM((2, rows, cols), jnp.float32),
+        ]
+        + [bf16((n_x,) + part)] * 3
         + [bf16((slots,) + part)] * 3
         + [
             bf16((3, slots) + part),
@@ -455,11 +547,11 @@
             dma((rounds,)),
             dma((rounds,)),
             dma((rounds, n_dp)),
-            dma((rounds, per_row, n_dp)),
-            dma((rounds, per_row, n_dp)),
-            dma((rounds, per_row, n_dp)),
-            dma((rounds, per_row, n_dp)),
-            dma((rounds, per_row, n_dp)),
+            dma((rounds, per_row, n_dp, 2)),
+            dma((rounds, per_row, n_dp, 2)),
+            dma((rounds, per_row, n_dp, 2)),
+            dma((rounds, per_row, n_dp, 2)),
+            dma((rounds, per_row, n_dp, 2)),
             dma((rounds, n_dp)),
             dma((rounds, n_dp)),
             dma((rounds, n_dp)),
@@ -470,65 +562,39 @@
             dma((3, slots)),
             dma((3, n_x)),
             dma((3, n_x)),
+            dma((3,)),
         ],
         compiler_params=pltpu.CompilerParams(
-            collective_id=n_cross, has_side_effects=True, vmem_limit_bytes=56 * 1024 * 1024
+            collective_id=crossings(n_x).index(counts), has_side_effects=True, vmem_limit_bytes=56 * 1024 * 1024
         ),
         cost_estimate=pl.CostEstimate(
             flops=flops, bytes_accessed=8 * rows * cols * 4, transcendentals=0
         ),
-        name=f"exploit_{n_cross}",
-    )(table, xt, weights, first_moment, second_moment, factor)
-
-
-def plan(ranking, side):
-    members = ranking.shape[0]
-    n_x = members // 2
-    ids = jnp.arange(members, dtype=jnp.int32)
-    placed = (ranking[:, None] == ids[None, :]).astype(jnp.int32)
-    from_rank = jnp.concatenate([ranking[:n_x], ranking[:n_x]])
-    source = jnp.sum(placed * from_rank[:, None], axis=0)
-    loser = jnp.sum(placed[n_x:], axis=0)
-    crosses = (source // n_x != ids // n_x).astype(jnp.int32)
-    before = (ids[:, None] < ids[None, :]) & (ids[:, None] // n_x == ids[None, :] // n_x)
-    slot = jnp.sum(crosses[:, None] * before, axis=0)
-    n_cross = jnp.maximum(jnp.sum(crosses[:n_x]), jnp.sum(crosses[n_x:]))
-    picks = jnp.where(crosses > 0, n_x + slot, source % n_x)
-    use = (crosses > 0) & (ids // n_x != side)
-    sends = jnp.sum(
-        jnp.where(use[None, :] & (slot[None, :] == ids[:n_x, None]), source % n_x, 0), axis=1
-    )
-    mine = jnp.where(side > 0, picks[n_x:], picks[:n_x])
-    return loser, n_cross, jnp.concatenate([sends, mine])
+        name="exploit_%d_%d" % counts,
+    )(ranking, choice, activations, cotangent, weights, first, second)
+
+
+def crossings(n_x):
+    return [
+        (winners - stay, n_x - winners - stay)
+        for winners in range(n_x + 1)
+        for stay in range(min(winners, n_x - winners) + 1)
+    ]
 
 
 def per_device(ranking, factor_index, weights, first_moment, second_moment, activations, cotangent):
-    members = lax.axis_size("pop")
-    member = lax.axis_index("pop")
-    loser, n_cross, table = plan(ranking, member // (members // 2))
-    is_loser = jnp.sum(jnp.where(jnp.arange(members) == member, loser, 0)) > 0
-    levels = jnp.array(rate_levels, jnp.float32)
-    own_index = jnp.take(factor_index, member, axis=0)
-    chosen = jnp.sum(
-        jnp.where(own_index[..., None] == jnp.arange(3, dtype=jnp.int32), levels, 0.0), axis=-1
-    )
-    row_count = weights.shape[2]
-    head_count = factor_index.shape[2]
-    global_rows = lax.axis_index("tensor") * row_count + jnp.arange(row_count, dtype=jnp.int32)
-    row_heads = global_rows // HEAD_SIZE
-    onehot = (row_heads[:, None] == jnp.arange(head_count, dtype=jnp.int32)[None, :]).astype(
-        jnp.float32
-    )
-    row_factor = jnp.sum(chosen[:, None, :] * onehot[None, :, :], axis=2)
-    factor = jnp.where(is_loser, row_factor, 1.0)[:, :, None]
-
-    block = activations.shape[2]
-    both = jnp.stack([activations[0], cotangent[0]])
-    own = both.reshape(2, 2, HALF, block).transpose(1, 0, 3, 2)
+    n_x = lax.axis_size("pop") // 2
+    cases = crossings(n_x)
+    winner, loser = ranking[:n_x] // n_x, ranking[n_x:] // n_x
+    there, back = jnp.sum(winner < loser), jnp.sum(winner > loser)
+    case = sum(
+        jnp.where((there == a) & (back == b), n, 0) for n, (a, b) in enumerate(cases)
+    ).astype(jnp.int32)
     step = lax.switch(
-        n_cross,
-        [functools.partial(exploit_step, k) for k in range(members // 2 + 1)],
-        table, own, weights[0], first_moment[0], second_moment[0], factor,
+        case,
+        [functools.partial(exploit_step, counts) for counts in cases],
+        ranking, factor_index.reshape(-1), activations[0], cotangent[0],
+        weights[0], first_moment[0], second_moment[0],
     )
     return step[None]
 

time: 266 us -> 193 us (0.73); the launches traced: 266 us -> 190 us
  Pallas kernels: 254 us -> 178 us
  other arithmetic: 6.8 us -> 1.52 us
  between operations: 1.41 us -> 6.1 us
    pallas_call x1, Pallas kernels: 254 us -> 178 us  [exploit_step(): pl.pallas_call(functools.partial(kernel, counts, n_pop, n_dp, n_tensor, c...]
where the time goes in v3:
time: 193 us; the launch traced here: 190 us
  Pallas kernels  178 us (92%)
  between operations  6.1 us (3%)
  local copies, waits for them, and re-layouts  3.84 us (2%)
    pallas_call x1, Pallas kernels, exploit_step(): pl.pallas_call(functools.partial(kernel, counts, n_pop, n_dp, n_tensor, c...  178 us

profile of v3, /device:TPU:6, one launch (start us, length us, event | category | flops | bytes accessed | tf_op | source)
XLA Modules:
  0.0 190.1 jit_solution(10300170343906627962)
XLA Ops:
  0.0 0.8 and_select_fusion
  0.8 0.7 fusion.1
  7.6 0.8 reshape.3
  8.4 1.1 copy.17
  9.5 1.1 copy.18
  10.6 178.6 %conditional.1 = (bf16[1,2,160,1280]{3,2,1,0:T(8,128)(2,1)S(1)}) conditional(s32[]{:T(128)} %clamp.3, (s32[8]{0:T(128)}, s32[320]{0:T(512)S(1)}, bf16[256,320]{1,0:T(8,128)(2,1)S(1)}, bf16[256,320]{1,0:T(8,128)(2,1)S(1)}, bf16[2,160,1280]{2,1,0:T(8,128)(2,1)}, /*index=5*/f32[2,160,1280]{2,1,0:T(8,128)}, ...), branch_computations={%region_2.3_spmd, %region_3.4_spmd, %region_4.5_spmd, %region_5.6_... | conditional | flops 1677721600 | bytes 6553608 | solution.py:593
  10.9 178.0 %exploit_1_1.1 = bf16[2,160,1280]{2,1,0:T(8,128)(2,1)S(1)} custom-call(s32[8]{0:T(128)} %get-tuple-element.170.rank_ref, s32[320]{0:T(512)S(1)} %get-tuple-element.171.choice_ref, bf16[256,320]{1,0:T(8,128)(2,1)S(1)} %get-tuple-element.172.act_ref, bf16[256,320]{1,0:T(8,128)(2,1)S(1)} %get-tuple-element.173.cot_ref, ...), custom_call_target="tpu_custom_call" | custom-call | flops 1677721600 | bytes 6553600 | tf_op jit(solution)/shard_map/cond/branch_4_fun/exploit_1_1/pallas_call | solution.py:522
  189.2 0.9 copy.29
